TPU v7x, 512 devices: a whole 4x4x16 slice. The times are simulated.
512 devices in a mesh: replica: 16 (over z_lo, core), fsdp: 32 (over y, z_hi, x).
Axes of the slice: x: 4, y: 4, z: 16 (z_hi: 2, z_lo: 8; z = z_hi * 8 + z_lo), core: 2. Of those that a mesh axis runs over, the one named last changes fastest.
Arguments:
- gradients: bfloat16 [16, 1024, 5120], P('replica', 'fsdp'), may hold values from -150 to 150
- replica_weight: float32 [16], replicated, may hold values from 0.5 to 2
- params: float32 [1024, 5120], P('fsdp'), may hold values from -3 to 3
- first_moment: float32 [1024, 5120], P('fsdp'), may hold values from -3 to 3
- second_moment: float32 [1024, 5120], P('fsdp'), may hold values from 0.05 to 4
Outputs:
- median: float32 [1024, 5120], P('fsdp')
- new_params: float32 [1024, 5120], P('fsdp')
- new_first: float32 [1024, 5120], P('fsdp')
- new_second: float32 [1024, 5120], P('fsdp')
All inputs are finite; a program needn't handle non-finite values.
Results may differ from a plain program's by a relative error of at most 0.0003.
Values may be sent and summed in bfloat16 or wider, within the bound.
A program may use at most 64 MiB of HBM per device.

v0:
```python
import jax
import jax.numpy as jnp
from jax import lax
from jax.sharding import PartitionSpec as P

ITERS = 4
STEP = 100


smooth_floor = 0.05
beta_first = 0.9
beta_second = 0.95
learn_rate = 0.001
decay_rate = 0.1
adam_epsilon = 1e-08


def body(gradients, replica_weight, params, first_moment, second_moment):
    rows_here = gradients.shape[1]
    width = gradients.shape[2]
    entries = rows_here * lax.axis_size("fsdp") * width
    own_grad = gradients[0]
    replica_index = lax.axis_index("replica")
    own_weight = lax.dynamic_slice_in_dim(replica_weight, replica_index, 1, 0)[0]

    def pooled_rows(weight):
        summed, weight_total = lax.psum((weight * own_grad.astype(jnp.float32), weight), "replica")
        return summed / weight_total

    median = pooled_rows(own_weight)
    for iteration in range(ITERS):
        partial_value = jnp.sum(jnp.square(own_grad.astype(jnp.float32) - median))
        squared = lax.psum(partial_value, "fsdp")
        distance = jnp.sqrt(squared / entries)
        median = pooled_rows(own_weight / jnp.maximum(distance, smooth_floor))
    new_first = beta_first * first_moment + (1.0 - beta_first) * median
    new_second = beta_second * second_moment + (1.0 - beta_second) * median * median
    first_hat = new_first / (1.0 - beta_first**STEP)
    second_hat = new_second / (1.0 - beta_second**STEP)
    new_params = params - learn_rate * (
        first_hat / (jnp.sqrt(second_hat) + adam_epsilon) + decay_rate * params
    )
    return (median, new_params, new_first, new_second)


def solution(mesh):
    return jax.shard_map(
        body,
        mesh=mesh,
        in_specs=(
            P("replica", "fsdp", None),
            P(),
            P("fsdp", None),
            P("fsdp", None),
            P("fsdp", None),
        ),
        out_specs=(P("fsdp", None), P("fsdp", None), P("fsdp", None), P("fsdp", None)),
        check_vma=False,
    )
```

profile of v0, /device:TPU:1, one launch (start us, length us, event | category | flops | bytes accessed | tf_op | source)
XLA Modules:
  0.0 1624.7 jit_solution(13540696299415080545)
XLA Ops:
  7.2 0.0 all-reduce.6.cloned.1.call-start
  7.2 0.0 copy-start.4
  7.2 0.6 copy-done.4
  7.9 0.6 dynamic_slice.3
  8.5 2.5 convert_multiply_fusion.4
  11.0 0.0 copy-start
  11.0 0.0 all-reduce.6.cloned.1.call-update
  11.0 0.0 all-reduce.8.cloned.1.call-start
  11.0 52.0 %psum.99 = f32[]{:T(128)} all-reduce(f32[]{:T(128)} %bitcast), channel_id=1, replica_groups=mesh['replica'=16,'fsdp'=32] {'replica'}, use_global_device_ids=true, to_apply=%region_1.0 | all-reduce | flops 1 | bytes 8 | tf_op jit(solution)/shard_map/psum | solution.py:27
  63.1 151.6 %all-reduce.6.cloned.1.call-done = f32[32,5120]{1,0:T(8,128)} async-done(((f32[32,5120]{1,0:T(8,128)}), f32[32,5120]{1,0:T(8,128)}) %all-reduce.6.cloned.1.call-update) | async-done | bytes 655376 | tf_op jit(solution)/shard_map/psum | solution.py:27
  214.6 0.0 copy-done
  214.6 2.5 fusion.2
  217.1 140.8 %psum.100 = f32[]{:T(128)} all-reduce(f32[]{:T(128)} %fusion.2), channel_id=1, replica_groups=mesh['replica'=16,'fsdp'=32] {'fsdp'}, use_global_device_ids=true, to_apply=%region_3.0 | all-reduce | flops 1 | bytes 8 | tf_op jit(solution)/shard_map/psum | solution.py:33
  359.3 0.9 convert_multiply_fusion.3
  360.2 0.0 all-reduce.8.cloned.1.call-update
  360.2 0.0 all-reduce.10.cloned.1.call-start
  360.3 66.2 %psum.102 = f32[]{:T(128)} all-reduce(f32[]{:T(128)S(6)} %div.72), channel_id=1, replica_groups=mesh['replica'=16,'fsdp'=32] {'replica'}, use_global_device_ids=true, to_apply=%region_5.0 | all-reduce | flops 1 | bytes 8 | tf_op jit(solution)/shard_map/psum | solution.py:27
  426.5 138.2 %all-reduce.8.cloned.1.call-done = f32[32,5120]{1,0:T(8,128)} async-done(((f32[32,5120]{1,0:T(8,128)}), f32[32,5120]{1,0:T(8,128)}) %all-reduce.8.cloned.1.call-update) | async-done | bytes 655376 | tf_op jit(solution)/shard_map/psum | solution.py:27
  564.7 2.5 fusion.4
  567.2 140.8 %psum.103 = f32[]{:T(128)} all-reduce(f32[]{:T(128)} %fusion.4), channel_id=1, replica_groups=mesh['replica'=16,'fsdp'=32] {'fsdp'}, use_global_device_ids=true, to_apply=%region_7.0 | all-reduce | flops 1 | bytes 8 | tf_op jit(solution)/shard_map/psum | solution.py:33
  709.4 0.9 convert_multiply_fusion.2
  710.3 0.0 all-reduce.10.cloned.1.call-update
  710.3 0.0 all-reduce.12.cloned.1.call-start
  710.3 66.2 %psum.105 = f32[]{:T(128)} all-reduce(f32[]{:T(128)S(6)} %div.76), channel_id=1, replica_groups=mesh['replica'=16,'fsdp'=32] {'replica'}, use_global_device_ids=true, to_apply=%region_9.0 | all-reduce | flops 1 | bytes 8 | tf_op jit(solution)/shard_map/psum | solution.py:27
  776.5 138.2 %all-reduce.10.cloned.1.call-done = f32[32,5120]{1,0:T(8,128)} async-done(((f32[32,5120]{1,0:T(8,128)}), f32[32,5120]{1,0:T(8,128)}) %all-reduce.10.cloned.1.call-update) | async-done | bytes 655376 | tf_op jit(solution)/shard_map/psum | solution.py:27
  914.7 2.5 fusion.6
  917.2 140.8 %psum.106 = f32[]{:T(128)} all-reduce(f32[]{:T(128)} %fusion.6), channel_id=1, replica_groups=mesh['replica'=16,'fsdp'=32] {'fsdp'}, use_global_device_ids=true, to_apply=%region_11.0 | all-reduce | flops 1 | bytes 8 | tf_op jit(solution)/shard_map/psum | solution.py:33
  1059.4 0.9 convert_multiply_fusion.1
  1060.3 0.0 all-reduce.12.cloned.1.call-update
  1060.3 0.0 all-reduce.14.cloned.1.call-start
  1060.4 66.2 %psum.108 = f32[]{:T(128)} all-reduce(f32[]{:T(128)S(6)} %div.80), channel_id=1, replica_groups=mesh['replica'=16,'fsdp'=32] {'replica'}, use_global_device_ids=true, to_apply=%region_13.0 | all-reduce | flops 1 | bytes 8 | tf_op jit(solution)/shard_map/psum | solution.py:27
  1126.6 138.2 %all-reduce.12.cloned.1.call-done = f32[32,5120]{1,0:T(8,128)} async-done(((f32[32,5120]{1,0:T(8,128)}), f32[32,5120]{1,0:T(8,128)}) %all-reduce.12.cloned.1.call-update) | async-done | bytes 655376 | tf_op jit(solution)/shard_map/psum | solution.py:27
  1264.7 0.0 copy-start.3
  1264.8 2.6 fusion.8
  1267.3 140.8 %psum.109 = f32[]{:T(128)} all-reduce(f32[]{:T(128)} %fusion.8), channel_id=1, replica_groups=mesh['replica'=16,'fsdp'=32] {'fsdp'}, use_global_device_ids=true, to_apply=%region_15.0 | all-reduce | flops 1 | bytes 8 | tf_op jit(solution)/shard_map/psum | solution.py:33
  1409.5 0.0 copy-start.1
  1409.5 0.0 copy-start.2
  1409.5 0.9 convert_multiply_fusion
  1410.4 0.0 all-reduce.14.cloned.1.call-update
  1410.4 66.2 %psum.111 = f32[]{:T(128)} all-reduce(f32[]{:T(128)S(6)} %div.84), channel_id=1, replica_groups=mesh['replica'=16,'fsdp'=32] {'replica'}, use_global_device_ids=true, to_apply=%region_17.0 | all-reduce | flops 1 | bytes 8 | tf_op jit(solution)/shard_map/psum | solution.py:27
  1476.7 138.2 %all-reduce.14.cloned.1.call-done = f32[32,5120]{1,0:T(8,128)} async-done(((f32[32,5120]{1,0:T(8,128)}), f32[32,5120]{1,0:T(8,128)}) %all-reduce.14.cloned.1.call-update) | async-done | bytes 655376 | tf_op jit(solution)/shard_map/psum | solution.py:27
  1614.9 0.0 copy-done.3
  1614.9 0.0 copy-done.1
  1614.9 0.0 copy-done.2
  1614.9 3.3 multiply_subtract_fusion
Async XLA Ops:
  7.2 207.5 %all-reduce.6.cloned.1.call-start = ((), (), s32[]{:S(2)}) async-start(), calls=%async_computation | async-start | bytes 1310720 | tf_op jit(solution)/shard_map/psum | solution.py:27
  7.2 0.7 copy-start.4
  11.0 203.7 %copy-start = (bf16[1,32,5120]{2,1,0:T(8,128)(2,1)S(1)}, bf16[1,32,5120]{2,1,0:T(8,128)(2,1)}, u32[]{:S(2)}) copy-start(bf16[1,32,5120]{2,1,0:T(8,128)(2,1)} %param.5) | copy-start | bytes 983044
  11.0 553.7 %all-reduce.8.cloned.1.call-start = ((), (), s32[]{:S(2)}) async-start(), calls=%async_computation.1 | async-start | bytes 1310720 | tf_op jit(solution)/shard_map/psum | solution.py:27
  360.2 554.5 %all-reduce.10.cloned.1.call-start = ((), (), s32[]{:S(2)}) async-start(), calls=%async_computation.2 | async-start | bytes 1310720 | tf_op jit(solution)/shard_map/psum | solution.py:27
  710.3 554.5 %all-reduce.12.cloned.1.call-start = ((), (), s32[]{:S(2)}) async-start(), calls=%async_computation.3 | async-start | bytes 1310720 | tf_op jit(solution)/shard_map/psum | solution.py:27
  1060.3 554.6 %all-reduce.14.cloned.1.call-start = ((), (), s32[]{:S(2)}) async-start(), calls=%async_computation.4 | async-start | bytes 1310720 | tf_op jit(solution)/shard_map/psum | solution.py:27
  1264.7 350.1 %copy-start.3 = (f32[32,5120]{1,0:T(8,128)S(1)}, f32[32,5120]{1,0:T(8,128)}, u32[]{:S(2)}) copy-start(f32[32,5120]{1,0:T(8,128)} %param.9) | copy-start | bytes 1966084
  1409.5 205.4 %copy-start.1 = (f32[32,5120]{1,0:T(8,128)S(1)}, f32[32,5120]{1,0:T(8,128)}, u32[]{:S(2)}) copy-start(f32[32,5120]{1,0:T(8,128)} %param.7) | copy-start | bytes 1966084
  1409.5 205.4 %copy-start.2 = (f32[32,5120]{1,0:T(8,128)S(1)}, f32[32,5120]{1,0:T(8,128)}, u32[]{:S(2)}) copy-start(f32[32,5120]{1,0:T(8,128)} %param.8) | copy-start | bytes 1966084
Sparse Core Ops, SparseCore 0:
  11.5 203.1 all-reduce.5
  360.4 204.2 all-reduce.7
  710.4 204.2 all-reduce.9
  1060.4 204.2 all-reduce.11
  1410.6 204.2 all-reduce.13
where the time goes:
time: 1630 us; the launch traced here: 1620 us
  blocking collectives  880 us (54%)
  waiting for transfers between devices  704 us (43%)
  other arithmetic  19.5 us (1%)
  between operations  19.2 us (1%)
    psum x5, waiting for transfers between devices, pooled_rows(): lax.psum((weight * own_grad.astype(jnp.float32), weight), 'replica')  704 us
    psum x4, blocking collectives, body(): squared = lax.psum(partial_value, 'fsdp')  563 us
    psum x5, blocking collectives, pooled_rows(): lax.psum((weight * own_grad.astype(jnp.float32), weight), 'replica')  317 us
  transfers between devices with their start and end apart: 5, of which 5 were waited for; matrix products, arithmetic and copies ran while one was open for 0% of the time, Pallas kernels for 0%

commit v1 on v0

v1 whole, which is shorter than its diff:
```python
import functools

import jax
import jax.numpy as jnp
from jax import lax
from jax.experimental import pallas as pl
from jax.experimental.pallas import tpu as pltpu
from jax.sharding import PartitionSpec as P

ITERS = 4
STEP = 100

smooth_floor = 0.05
beta_first = 0.9
beta_second = 0.95
learn_rate = 0.001
decay_rate = 0.1
adam_epsilon = 1e-08

MESH = pl.DeviceIdType.MESH
LANES = 128


def packed_gram(block, groups, rows):
    product = lax.dot_general(block, block, (((1,), (1,)), ((), ())), preferred_element_type=jnp.float32)
    size = groups * rows
    row = lax.broadcasted_iota(jnp.int32, (size, size), 0)
    column = lax.broadcasted_iota(jnp.int32, (size, size), 1)
    same = lax.rem(row, rows) == lax.rem(column, rows)
    by_group = jnp.sum(jnp.where(same, product, 0.0).reshape(groups, rows, size), axis=1)
    lane = lax.broadcasted_iota(jnp.int32, (groups, LANES), 1)
    low, high = by_group[:, :LANES], by_group[:, LANES:]
    low, high = low + pltpu.roll(low, LANES - 8, 1), high + pltpu.roll(high, 8, 1)
    half = jnp.where(lax.rem(lane, 16) < 8, low, high)
    low, high = half[:8], half[8:]
    low, high = low + pltpu.roll(low, LANES - 4, 1), high + pltpu.roll(high, 4, 1)
    return jnp.where(lax.rem(lane[:8], 8) < 4, low, high)


def median_weights(packed, weight_ref, groups, entries):
    lane = lax.broadcasted_iota(jnp.int32, (groups, LANES), 1)
    sub = lax.broadcasted_iota(jnp.int32, (groups, LANES), 0)
    lane_group = lax.div(lane, 16) + 8 * lax.div(lax.rem(lane, 16), 8)
    here = lax.div(lax.rem(lane, 8), 4) == lax.div(sub, 8)
    gram = jnp.where(here, jnp.concatenate([packed, packed], axis=0), 0.0) * (1.0 / entries)
    own_lane = lane_group == sub
    given = jnp.zeros((groups, LANES), jnp.float32)
    for group in range(groups):
        given = jnp.where(sub == group, weight_ref[group], given)
    norm = jnp.sum(jnp.where(own_lane, gram, 0.0), axis=1, keepdims=True)
    weight = given
    for iteration in range(ITERS + 1):
        weight = weight / jnp.sum(weight, axis=0, keepdims=True)
        if iteration == ITERS:
            break
        along_lanes = jnp.sum(jnp.where(own_lane, weight, 0.0), axis=0, keepdims=True)
        product = jnp.sum(gram * along_lanes, axis=1, keepdims=True)
        squared = norm - 2.0 * product + jnp.sum(weight * product, axis=0, keepdims=True)
        weight = given / jnp.maximum(jnp.sqrt(jnp.maximum(squared, 0.0)), smooth_floor)
    return weight


def kernel(
    groups, row_parts, entries, grad_ref, weight_ref, out_ref, held, small, first_slots, second_slots,
    here_sem, held_send, held_recv, first_send, first_recv, second_send, second_recv,
    chip_send, chip_recv, core_send, core_recv,
):
    replica = lax.axis_index("replica")
    fsdp = lax.axis_index("fsdp")
    chips = groups // 2
    chip, core = lax.div(replica, 2), lax.rem(replica, 2)
    rows = grad_ref.shape[0] // 2
    wide = grad_ref.shape[1] // chips

    def peer(distance):
        return lax.rem(replica + distance, groups)

    def row_peer(distance):
        return lax.rem(fsdp + distance, row_parts)

    barrier = pltpu.get_barrier_semaphore()

    @pl.loop(1, groups)
    def _(distance):
        pl.semaphore_signal(barrier, inc=1, device_id={"replica": peer(distance)}, device_id_type=MESH)

    @pl.loop(1, row_parts)
    def _(distance):
        pl.semaphore_signal(barrier, inc=1, device_id={"fsdp": row_peer(distance)}, device_id_type=MESH)

    pl.semaphore_wait(barrier, groups - 1 + row_parts - 1)

    def part_of(ref, owner_chip, owner_core):
        return ref.at[
            pl.ds(pl.multiple_of(owner_core * rows, rows), rows),
            pl.ds(pl.multiple_of(owner_chip * wide, wide), wide),
        ]

    def held_slot(group):
        return held.at[pl.ds(pl.multiple_of(group * rows, rows), rows), :]

    @pl.loop(1, groups)
    def _(distance):
        to = peer(distance)
        pltpu.make_async_remote_copy(
            src_ref=part_of(grad_ref, lax.div(to, 2), lax.rem(to, 2)),
            dst_ref=held_slot(replica),
            send_sem=held_send,
            recv_sem=held_recv,
            device_id={"replica": to},
            device_id_type=MESH,
        ).start()

    pltpu.make_async_copy(part_of(grad_ref, chip, core), held_slot(replica), held_recv).start()
    pltpu.make_async_copy(held, held, held_recv).wait()

    small[...] = packed_gram(held[...], groups, rows)

    @pl.loop(1, groups)
    def _(distance):
        pltpu.make_async_remote_copy(
            src_ref=small,
            dst_ref=first_slots.at[replica],
            send_sem=first_send,
            recv_sem=first_recv,
            device_id={"replica": peer(distance)},
            device_id_type=MESH,
        ).start()

    pltpu.make_async_copy(small, first_slots.at[replica], first_recv).start()
    pltpu.make_async_copy(first_slots, first_slots, first_recv).wait()
    rest = first_slots.at[pl.ds(0, groups - 1)]
    pltpu.make_async_copy(rest, rest, first_send).wait()
    small[...] = jnp.sum(first_slots[...], axis=0)

    @pl.loop(1, row_parts)
    def _(distance):
        pltpu.make_async_remote_copy(
            src_ref=small,
            dst_ref=second_slots.at[fsdp],
            send_sem=second_send,
            recv_sem=second_recv,
            device_id={"fsdp": row_peer(distance)},
            device_id_type=MESH,
        ).start()

    pltpu.make_async_copy(small, second_slots.at[fsdp], second_recv).start()
    pltpu.make_async_copy(second_slots, second_slots, second_recv).wait()
    weights = median_weights(jnp.sum(second_slots[...], axis=0), weight_ref, groups, entries)

    total = jnp.zeros((rows, wide), jnp.float32)
    for group in range(groups):
        total += weights[group : group + 1, :1] * held[group * rows : (group + 1) * rows, :].astype(jnp.float32)
    part_of(out_ref, chip, core)[...] = total

    sibling = {"replica": chip * 2 + 1 - core}
    beside = chip + 1 - 2 * lax.rem(chip, 2)
    parity = lax.rem(chip, 2)
    pairs = chips // 2

    def to_chip(from_chip, target):
        return pltpu.make_async_remote_copy(
            src_ref=part_of(out_ref, from_chip, core),
            dst_ref=part_of(out_ref, from_chip, core),
            send_sem=chip_send.at[from_chip],
            recv_sem=chip_recv.at[from_chip],
            device_id={"replica": target * 2 + core},
            device_id_type=MESH,
        )

    def to_core(from_chip, from_core):
        return pltpu.make_async_remote_copy(
            src_ref=part_of(out_ref, from_chip, from_core),
            dst_ref=part_of(out_ref, from_chip, from_core),
            send_sem=core_send.at[from_chip],
            recv_sem=core_recv.at[from_chip],
            device_id=sibling,
            device_id_type=MESH,
        )

    def far(step):
        return lax.rem(lax.div(chip, 2) + step, pairs) * 2 + parity

    for step in range(1, pairs):
        pltpu.make_async_remote_copy(
            src_ref=part_of(out_ref, chip, core),
            dst_ref=part_of(out_ref, chip, core),
            send_sem=here_sem.at[step],
            recv_sem=chip_recv.at[chip],
            device_id={"replica": far(step) * 2 + core},
            device_id_type=MESH,
        ).start()
    to_chip(chip, beside).start()
    to_core(chip, core).start()

    for step in range(1, pairs):
        origin = far(pairs - step)
        to_chip(origin, beside).wait_recv()
        to_chip(origin, beside).start()
        to_core(origin, core).start()
    for step in range(pairs):
        origin = lax.rem(lax.div(chip, 2) + step, pairs) * 2 + 1 - parity
        to_chip(origin, beside).wait_recv()
        to_core(origin, core).start()
    for origin in range(chips):
        to_core(origin, 1 - core).wait_recv()

    for origin in range(chips):
        to_core(origin, core).wait_send()
    for step in range(pairs):
        to_chip(far(step), beside).wait_send()
    for step in range(1, pairs):
        pltpu.make_async_remote_copy(
            src_ref=part_of(out_ref, chip, core),
            dst_ref=part_of(out_ref, chip, core),
            send_sem=here_sem.at[step],
            recv_sem=chip_recv.at[chip],
            device_id={"replica": far(step) * 2 + core},
            device_id_type=MESH,
        ).wait_send()
    sent = held.at[pl.ds(0, (groups - 1) * rows), :]
    pltpu.make_async_copy(sent, sent, held_send).wait()
    rest = second_slots.at[pl.ds(0, row_parts - 1)]
    pltpu.make_async_copy(rest, rest, second_send).wait()


def body(groups, row_parts, gradients, replica_weight, params, first_moment, second_moment):
    rows_here, width = gradients.shape[1], gradients.shape[2]
    entries = rows_here * row_parts * width
    rows, wide, half = rows_here // 2, width // (groups // 2), groups // 2
    dma = pltpu.SemaphoreType.DMA
    median = pl.pallas_call(
        functools.partial(kernel, groups, row_parts, entries),
        out_shape=jax.ShapeDtypeStruct((rows_here, width), jnp.float32),
        in_specs=[pl.BlockSpec(memory_space=pl.ANY), pl.BlockSpec(memory_space=pltpu.SMEM)],
        out_specs=pl.BlockSpec(memory_space=pltpu.VMEM),
        scratch_shapes=[
            pltpu.VMEM((groups * rows, wide), jnp.bfloat16),
            pltpu.VMEM((half, LANES), jnp.float32),
            pltpu.VMEM((groups, half, LANES), jnp.float32),
            pltpu.VMEM((row_parts, half, LANES), jnp.float32),
            dma((half // 2,)),
            dma, dma, dma, dma, dma, dma,
            dma((half,)), dma((half,)), dma((half,)), dma((half,)),
        ],
        compiler_params=pltpu.CompilerParams(collective_id=0, has_side_effects=True),
        name="median_rows",
    )(gradients.reshape(rows_here, width), replica_weight)
    new_first = beta_first * first_moment + (1.0 - beta_first) * median
    new_second = beta_second * second_moment + (1.0 - beta_second) * median * median
    first_hat = new_first / (1.0 - beta_first**STEP)
    second_hat = new_second / (1.0 - beta_second**STEP)
    new_params = params - learn_rate * (
        first_hat / (jnp.sqrt(second_hat) + adam_epsilon) + decay_rate * params
    )
    return (median, new_params, new_first, new_second)


def solution(mesh):
    return jax.shard_map(
        functools.partial(body, mesh.shape["replica"], mesh.shape["fsdp"]),
        mesh=mesh,
        in_specs=(
            P("replica", "fsdp", None),
            P(),
            P("fsdp", None),
            P("fsdp", None),
            P("fsdp", None),
        ),
        out_specs=(P("fsdp", None), P("fsdp", None), P("fsdp", None), P("fsdp", None)),
        check_vma=False,
    )
```

time: 1630 us -> 68.6 us (0.04)
  blocking collectives: 880 us -> 0 us
  waiting for transfers between devices: 704 us -> 0 us
  Pallas kernels: 0 us -> 63.8 us
  between operations: 19.2 us -> 0.66 us
  other arithmetic: 19.5 us -> 3.12 us
    psum x9 -> x0, blocking collectives: 880 us -> none  [the longest x4 563 us: body(): squared = lax.psum(partial_value, 'fsdp')]
    psum x5 -> x0, waiting for transfers between devices: 704 us -> none  [pooled_rows(): lax.psum((weight * own_grad.astype(jnp.float32), weight), 'replica')]
    pallas_call x0 -> x1, Pallas kernels: none -> 63.8 us  [body(): pl.pallas_call(functools.partial(kernel, groups, row_parts, entries), out...]
  transfers between devices with their start and end apart: 5 -> 0, of which waited for: 5 -> 0; matrix products, arithmetic and copies ran while one was open for 0% -> 0% of each run, Pallas kernels for 0% -> 0%
where the time goes in v1:
time: 68.6 us; the launch traced here: 68.4 us
  Pallas kernels  63.8 us (93%)
  other arithmetic  3.12 us (5%)
  local copies, waits for them, and re-layouts  0.84 us (1%)
    pallas_call x1, Pallas kernels, body(): pl.pallas_call(functools.partial(kernel, groups, row_parts, entries), out...  63.8 us
    sub x1, other arithmetic, body(): params - learn_rate * (first_hat / (jnp.sqrt(second_hat) + adam_epsilon)...  3.12 us

profile of v1, /device:TPU:1, one launch (start us, length us, event | category | flops | bytes accessed | tf_op | source)
XLA Modules:
  0.0 68.4 jit_solution(17094835190921138741)
XLA Ops:
  0.6 0.0 copy-start.1
  0.6 63.8 %median_rows.1 = f32[32,5120]{1,0:T(8,128)} custom-call(bf16[32,5120]{1,0:T(8,128)(2,1)} %bitcast.1, f32[16]{0:T(128)} %weight_ref.1), custom_call_target="tpu_custom_call" | custom-call | tf_op jit(solution)/shard_map/median_rows/pallas_call | solution.py:232
  64.4 0.0 copy-done.1
  64.4 0.0 copy-start
  64.4 3.1 %multiply_subtract_fusion = (f32[32,5120]{1,0:T(8,128)}, f32[32,5120]{1,0:T(8,128)}, f32[32,5120]{1,0:T(8,128)}) fusion(f32[32,5120]{1,0:T(8,128)S(1)} %copy-done.1, f32[32,5120]{1,0:T(8,128)} %median_rows.1, f32[32,5120]{1,0:T(8,128)} %param.8, f32[32,5120]{1,0:T(8,128)} %param.9), kind=kLoop, calls=%fused_computation.2 | loop fusion | flops 2457600 | bytes 4587520 | tf_op jit(solution)/shard_map/sub | solution.py:253
  67.6 0.0 copy-done
  67.6 0.8 %copy.10 = f32[32,5120]{1,0:T(8,128)} copy(f32[32,5120]{1,0:T(8,128)S(1)} %copy-done) | data formatting | bytes 1310720
Async XLA Ops:
  0.6 63.8 %copy-start.1 = (f32[32,5120]{1,0:T(8,128)S(1)}, f32[32,5120]{1,0:T(8,128)}, u32[]{:S(2)}) copy-start(f32[32,5120]{1,0:T(8,128)} %param.7) | copy-start | bytes 1966084
  64.4 3.1 %copy-start = (f32[32,5120]{1,0:T(8,128)S(1)}, f32[32,5120]{1,0:T(8,128)}, u32[]{:S(2)}) copy-start(f32[32,5120]{1,0:T(8,128)} %median_rows.1) | copy-start | bytes 1966084

commit v2 on v0

v2 whole, which is shorter than its diff:
```python
import functools
import math

import jax
import jax.numpy as jnp
from jax import lax
from jax.experimental import pallas as pl
from jax.experimental.pallas import tpu as pltpu
from jax.sharding import PartitionSpec as P

ITERS = 4
STEP = 100

smooth_floor = 0.05
beta_first = 0.9
beta_second = 0.95
learn_rate = 0.001
decay_rate = 0.1
adam_epsilon = 1e-08

MESH = pl.DeviceIdType.MESH
LANES = 128


def packed_gram(block, groups, rows):
    product = lax.dot_general(block, block, (((1,), (1,)), ((), ())), preferred_element_type=jnp.float32)
    size = groups * rows
    row = lax.broadcasted_iota(jnp.int32, (size, size), 0)
    column = lax.broadcasted_iota(jnp.int32, (size, size), 1)
    same = lax.rem(row, rows) == lax.rem(column, rows)
    by_group = jnp.sum(jnp.where(same, product, 0.0).reshape(groups, rows, size), axis=1)
    lane = lax.broadcasted_iota(jnp.int32, (groups, LANES), 1)

    def fold(low, high, step):
        low, high = low + pltpu.roll(low, LANES - step, 1), high + pltpu.roll(high, step, 1)
        return jnp.where(lax.rem(lane[: low.shape[0]], 2 * step) < step, low, high)

    folded = fold(by_group[:, :LANES], by_group[:, LANES:], 8)
    folded = fold(folded[:8], folded[8:], 4)
    folded = fold(folded[:4], folded[4:], 2)
    return fold(folded[:2], folded[2:], 1)


def median_weights(packed, weight_ref, groups, entries):
    lane = lax.broadcasted_iota(jnp.int32, (groups, LANES), 1)
    sub = lax.broadcasted_iota(jnp.int32, (groups, LANES), 0)
    lane_group = lax.div(lane, 16) + 8 * lax.div(lax.rem(lane, 16), 8)
    here = lax.rem(lane, 8) == lax.div(sub, 2)
    both = jnp.where(lax.rem(sub, 2) == 0, packed[:1], packed[1:])
    gram = jnp.where(here, both, 0.0) * (1.0 / entries)
    own_lane = lane_group == sub
    given = jnp.zeros((groups, LANES), jnp.float32)
    for group in range(groups):
        given = jnp.where(sub == group, weight_ref[group], given)
    norm = jnp.sum(jnp.where(own_lane, gram, 0.0), axis=1, keepdims=True)
    weight = given
    for iteration in range(ITERS + 1):
        weight = weight / jnp.sum(weight, axis=0, keepdims=True)
        if iteration == ITERS:
            break
        along_lanes = jnp.sum(jnp.where(own_lane, weight, 0.0), axis=0, keepdims=True)
        product = jnp.sum(gram * along_lanes, axis=1, keepdims=True)
        squared = norm - 2.0 * product + jnp.sum(weight * product, axis=0, keepdims=True)
        weight = given / jnp.maximum(jnp.sqrt(jnp.maximum(squared, 0.0)), smooth_floor)
    return weight


def kernel(
    chips, grid, entries, grad_ref, weight_hbm, params_hbm, first_hbm, second_hbm,
    out_ref, params_ref, first_ref, second_ref,
    weight_ref, held, core_small, plane_small, ring_small, core_slot, plane_slots, ring_slots,
    up, down, beside_sem, near_row, next_row, far_row,
    weight_sem, copy_sem, held_send, held_recv, core_sem, core_sum_recv,
    plane_send, plane_recv, ring_send, ring_recv,
    far_send, chip_send, chip_recv, core_send, core_recv,
):
    rows_y, runs, rows_x = grid
    groups, plane, ring = 2 * chips, rows_x * rows_y, runs * chips
    replica, fsdp = lax.axis_index("replica"), lax.axis_index("fsdp")
    chip, core = lax.div(replica, 2), lax.rem(replica, 2)
    x, run, y = lax.rem(fsdp, rows_x), lax.rem(lax.div(fsdp, rows_x), runs), lax.div(fsdp, rows_x * runs)
    z = run * chips + chip
    rows = grad_ref.shape[0] // 2
    wide = grad_ref.shape[1] // chips

    def device(dz=0, dy=0, dx=0, other=False):
        to_z = lax.rem(z + dz + ring, ring)
        to_y = lax.rem(y + dy + rows_y, rows_y)
        to_x = lax.rem(x + dx + rows_x, rows_x)
        return {
            "replica": lax.rem(to_z, chips) * 2 + (1 - core if other else core),
            "fsdp": (to_y * runs + lax.div(to_z, chips)) * rows_x + to_x,
        }

    def steps(size):
        return {1: (), 2: (1,)}.get(size, (1, -1))

    def tell(sem, to):
        pl.semaphore_signal(sem, inc=1, device_id=to, device_id_type=MESH)

    def send(src, dst, send_sem, recv_sem, to):
        return pltpu.make_async_remote_copy(
            src_ref=src, dst_ref=dst, send_sem=send_sem, recv_sem=recv_sem, device_id=to, device_id_type=MESH
        )

    def await_bytes(ref, sem):
        pltpu.make_async_copy(ref, ref, sem).wait()

    weight_copy = pltpu.make_async_copy(weight_hbm, weight_ref, weight_sem)
    weight_copy.start()

    barrier = pltpu.get_barrier_semaphore()
    greeted = [device(dz=dz, other=other) for dz in steps(ring) for other in (False, True)]
    greeted += [device(dy=dy) for dy in steps(rows_y)] + [device(dx=dx) for dx in steps(rows_x)]
    greeted += [device(other=True)]
    for to in greeted:
        tell(barrier, to)
    pl.semaphore_wait(barrier, len(greeted))

    def part_of(ref, owner_chip, owner_core):
        return ref.at[
            pl.ds(pl.multiple_of(owner_core * rows, rows), rows),
            pl.ds(pl.multiple_of(owner_chip * wide, wide), wide),
        ]

    own_held = held.at[pl.ds(pl.multiple_of(replica * rows, rows), rows), :]

    def send_part(to_chip, to_core):
        to = {"replica": to_chip * 2 + to_core}
        send(part_of(grad_ref, to_chip, to_core), own_held, held_send, held_recv, to).start()

    send_part(chip, 1 - core)
    pltpu.make_async_copy(part_of(grad_ref, chip, core), own_held, held_recv).start()

    for distance in range(1, ring // 2 + 1):
        if distance > 1:
            pl.semaphore_wait(up.at[distance], 1)
            if 2 * distance < ring:
                pl.semaphore_wait(down.at[distance], 1)
        if distance < ring // 2:
            tell(up.at[distance + 1], device(dz=1))
            if 2 * distance + 2 < ring:
                tell(down.at[distance + 1], device(dz=-1))
        if distance < chips:
            @pl.when(chip + distance < chips)
            def _():
                send_part(chip + distance, core)
                send_part(chip + distance, 1 - core)

            @pl.when(chip >= distance)
            def _():
                send_part(chip - distance, core)
                send_part(chip - distance, 1 - core)

    if rows_x > 2:
        tell(beside_sem, device(dx=1))
        pl.semaphore_wait(beside_sem, 1)
    for dy in steps(rows_y):
        tell(near_row if dy == 1 else next_row, device(dy=dy))
    for dy in steps(rows_y):
        pl.semaphore_wait(near_row if dy == 1 else next_row, 1)
    if rows_y > 2:
        tell(far_row, device(dy=1))
        pl.semaphore_wait(far_row, 1)

    kept = [
        pltpu.make_async_copy(params_hbm, params_ref, copy_sem.at[0]),
        pltpu.make_async_copy(first_hbm, first_ref, copy_sem.at[1]),
        pltpu.make_async_copy(second_hbm, second_ref, copy_sem.at[2]),
    ]
    for copy in kept:
        copy.start()
    weight_copy.wait()

    await_bytes(held, held_recv)
    core_small[...] = packed_gram(held[...], groups, rows)

    exchange = send(core_small, core_slot, core_sem, core_sum_recv, device(other=True))
    exchange.start()
    exchange.wait()
    plane_small[...] = core_small[...] + core_slot[...]

    if plane > 1:
        for step in range(1, plane):
            to = device(dx=step % rows_x, dy=step // rows_x)
            send(plane_small, plane_slots.at[y * rows_x + x], plane_send, plane_recv, to).start()
        pltpu.make_async_copy(plane_small, plane_slots.at[y * rows_x + x], plane_recv).start()
        await_bytes(plane_slots, plane_recv)
        ring_small[...] = jnp.sum(plane_slots[...], axis=0)
    else:
        ring_small[...] = plane_small[...]

    for step in range(1, ring):
        send(ring_small, ring_slots.at[z], ring_send, ring_recv, device(dz=step)).start()
    pltpu.make_async_copy(ring_small, ring_slots.at[z], ring_recv).start()
    await_bytes(ring_slots, ring_recv)
    weights = median_weights(jnp.sum(ring_slots[...], axis=0), weight_ref, groups, entries)

    total = jnp.zeros((rows, wide), jnp.float32)
    for group in range(groups):
        total += weights[group : group + 1, :1] * held[group * rows : (group + 1) * rows, :].astype(jnp.float32)
    part_of(out_ref, chip, core)[...] = total

    sibling = {"replica": chip * 2 + 1 - core}
    beside = chip + 1 - 2 * lax.rem(chip, 2)
    parity = lax.rem(chip, 2)
    pairs = chips // 2

    def far(step):
        return lax.rem(lax.div(chip, 2) + step, pairs) * 2 + parity

    def to_chip(origin, target, send_sem):
        part = part_of(out_ref, origin, core)
        return send(part, part, send_sem, chip_recv.at[origin], {"replica": target * 2 + core})

    def to_core(origin, origin_core):
        part = part_of(out_ref, origin, origin_core)
        return send(part, part, core_send.at[origin], core_recv.at[origin], sibling)

    for step in range(1, pairs):
        to_chip(chip, far(step), far_send.at[step]).start()
    to_chip(chip, beside, chip_send.at[chip]).start()
    to_core(chip, core).start()
    for step in range(1, pairs):
        origin = far(pairs - step)
        to_chip(origin, beside, chip_send.at[origin]).wait_recv()
        to_chip(origin, beside, chip_send.at[origin]).start()
        to_core(origin, core).start()
    for step in range(pairs):
        origin = far(step) + 1 - 2 * parity
        to_chip(origin, beside, chip_send.at[origin]).wait_recv()
        to_core(origin, core).start()
    for origin in range(chips):
        to_core(origin, 1 - core).wait_recv()

    for origin in range(chips):
        to_core(origin, core).wait_send()
    for step in range(pairs):
        to_chip(far(step), beside, chip_send.at[far(step)]).wait_send()
    for step in range(1, pairs):
        to_chip(chip, far(step), far_send.at[step]).wait_send()
    for copy in kept:
        copy.wait()
    await_bytes(held.at[pl.ds(0, (groups - 1) * rows), :], held_send)
    if plane > 1:
        await_bytes(plane_slots.at[pl.ds(0, plane - 1)], plane_send)
    await_bytes(ring_slots.at[pl.ds(0, ring - 1)], ring_send)


def update_kernel(
    median_ref, params_ref, first_ref, second_ref, median_hbm, params_hbm, first_hbm, second_hbm,
    params_new, first_new, second_new, median_sem, sems,
):
    median_copy = pltpu.make_async_copy(median_ref, median_hbm, median_sem)
    median_copy.start()
    rows, width = median_ref.shape
    cut = 8
    copies = []
    for part in range(rows // cut):
        at = pl.ds(part * cut, cut)
        median = median_ref[at, :]
        new_first = beta_first * first_ref[at, :] + (1.0 - beta_first) * median
        new_second = beta_second * second_ref[at, :] + (1.0 - beta_second) * median * median
        first_hat = new_first / (1.0 - beta_first**STEP)
        second_hat = new_second / (1.0 - beta_second**STEP)
        params = params_ref[at, :]
        params_new[at, :] = params - learn_rate * (
            first_hat / (jnp.sqrt(second_hat) + adam_epsilon) + decay_rate * params
        )
        first_new[at, :] = new_first
        second_new[at, :] = new_second
        for kind, (new, hbm) in enumerate(
            ((params_new, params_hbm), (first_new, first_hbm), (second_new, second_hbm))
        ):
            copy = pltpu.make_async_copy(new.at[at, :], hbm.at[at, :], sems.at[part, kind])
            copy.start()
            copies.append(copy)
    for copy in copies:
        copy.wait()
    median_copy.wait()


def body(chips, grid, gradients, replica_weight, params, first_moment, second_moment):
    rows_here, width = gradients.shape[1], gradients.shape[2]
    rows_y, runs, rows_x = grid
    groups, ring = 2 * chips, runs * chips
    entries = rows_here * rows_y * runs * rows_x * width
    rows, wide = rows_here // 2, width // chips
    dma, regular = pltpu.SemaphoreType.DMA, pltpu.SemaphoreType.REGULAR
    whole = jax.ShapeDtypeStruct((rows_here, width), jnp.float32)
    in_hbm = pl.BlockSpec(memory_space=pltpu.HBM)
    in_vmem = pl.BlockSpec(memory_space=pltpu.VMEM)
    small = pltpu.VMEM((2, LANES), jnp.float32)
    gathered = pl.pallas_call(
        functools.partial(kernel, chips, grid, entries),
        out_shape=(whole,) * 4,
        in_specs=[in_hbm] * 5,
        out_specs=(in_vmem,) * 4,
        scratch_shapes=[
            pltpu.SMEM((groups,), jnp.float32),
            pltpu.VMEM((groups * rows, wide), jnp.bfloat16),
            small, small, small, small,
            pltpu.VMEM((rows_x * rows_y, 2, LANES), jnp.float32),
            pltpu.VMEM((ring, 2, LANES), jnp.float32),
            regular((ring // 2 + 1,)), regular((ring // 2 + 1,)), regular, regular, regular, regular,
            dma, dma((3,)), dma, dma, dma, dma,
            dma, dma, dma, dma,
            dma((chips // 2,)), dma((chips,)), dma((chips,)), dma((chips,)), dma((chips,)),
        ],
        compiler_params=pltpu.CompilerParams(collective_id=0, has_side_effects=True, vmem_limit_bytes=51 * 1024 * 1024),
        name="median_rows",
    )(gradients.reshape(rows_here, width), replica_weight, params, first_moment, second_moment)
    kept = pltpu.VMEM((rows_here, width), jnp.float32)
    return pl.pallas_call(
        update_kernel,
        out_shape=(whole,) * 4,
        in_specs=[in_vmem] * 4,
        out_specs=(in_hbm,) * 4,
        scratch_shapes=[kept, kept, kept, dma, dma((rows_here // 8, 3))],
        compiler_params=pltpu.CompilerParams(vmem_limit_bytes=16 * 1024 * 1024),
        name="update",
    )(*gathered)


def solution(mesh):
    chips = mesh.shape["replica"] // 2
    side = math.isqrt(mesh.shape["fsdp"] // 2)
    return jax.shard_map(
        functools.partial(body, chips, (side, 2, side)),
        mesh=mesh,
        in_specs=(
            P("replica", "fsdp", None),
            P(),
            P("fsdp", None),
            P("fsdp", None),
            P("fsdp", None),
        ),
        out_specs=(P("fsdp", None), P("fsdp", None), P("fsdp", None), P("fsdp", None)),
        check_vma=False,
    )
```

time: 1630 us -> 64 us (0.04)
  blocking collectives: 880 us -> 0 us
  waiting for transfers between devices: 704 us -> 0 us
  Pallas kernels: 0 us -> 61.6 us
  other arithmetic: 19.5 us -> 0 us
  between operations: 19.2 us -> 0.65 us
    psum x9 -> x0, blocking collectives: 880 us -> none  [the longest x4 563 us: body(): squared = lax.psum(partial_value, 'fsdp')]
    psum x5 -> x0, waiting for transfers between devices: 704 us -> none  [pooled_rows(): lax.psum((weight * own_grad.astype(jnp.float32), weight), 'replica')]
    pallas_call x0 -> x2, Pallas kernels: none -> 61.6 us  [the longest x1 59.8 us: body(): pl.pallas_call(functools.partial(kernel, chips, grid, entries), out_shape...]
  transfers between devices with their start and end apart: 5 -> 0, of which waited for: 5 -> 0; matrix products, arithmetic and copies ran while one was open for 0% -> 0% of each run, Pallas kernels for 0% -> 0%
where the time goes in v2:
time: 64 us; the launch traced here: 63.8 us
  Pallas kernels  61.6 us (96%)
  local copies, waits for them, and re-layouts  1.62 us (3%)
  between operations  0.65 us (1%)
    pallas_call x1, Pallas kernels, body(): pl.pallas_call(functools.partial(kernel, chips, grid, entries), out_shape...  59.8 us
    pallas_call x1, Pallas kernels, body(): pl.pallas_call(update_kernel, out_shape=(whole,) * 4, in_specs=[in_vmem]...  1.73 us
    unnamed x4, local copies, waits for them, and re-layouts  1.62 us

profile of v2, /device:TPU:1, one launch (start us, length us, event | category | flops | bytes accessed | tf_op | source)
XLA Modules:
  0.0 63.8 jit_solution(11177284197606695431)
XLA Ops:
  0.6 0.0 copy-start.1
  0.6 0.6 %copy-done.1 = f32[16]{0:T(128)S(1)} copy-done((f32[16]{0:T(128)S(1)}, f32[16]{0:T(128)}, u32[]{:S(2)}) %copy-start.1) | copy-done | bytes 88
  1.3 0.0 copy-start
  1.3 1.0 %copy-done = bf16[1,32,5120]{2,1,0:T(8,128)(2,1)S(1)} copy-done((bf16[1,32,5120]{2,1,0:T(8,128)(2,1)S(1)}, bf16[1,32,5120]{2,1,0:T(8,128)(2,1)}, u32[]{:S(2)}) %copy-start) | copy-done | bytes 327704
  2.3 59.8 %median_rows.1 = (f32[32,5120]{1,0:T(8,128)S(1)}, f32[32,5120]{1,0:T(8,128)S(1)}, f32[32,5120]{1,0:T(8,128)S(1)}, f32[32,5120]{1,0:T(8,128)S(1)}) custom-call(bf16[32,5120]{1,0:T(8,128)(2,1)S(1)} %bitcast.1, f32[16]{0:T(128)S(1)} %copy-done.1, f32[32,5120]{1,0:T(8,128)} %params_hbm.1, f32[32,5120]{1,0:T(8,128)} %first_hbm.1, f32[32,5120]{1,0:T(8,128)} %second_hbm.1), custom_call_target="tpu_custom_call" | custom-call | tf_op jit(solution)/shard_map/median_rows/pallas_call | solution.py:294
  62.1 1.7 %update.1 = (f32[32,5120]{1,0:T(8,128)}, f32[32,5120]{1,0:T(8,128)}, f32[32,5120]{1,0:T(8,128)}, f32[32,5120]{1,0:T(8,128)}) custom-call(f32[32,5120]{1,0:T(8,128)S(1)} %get-tuple-element.8.median_ref, f32[32,5120]{1,0:T(8,128)S(1)} %get-tuple-element.9.params_ref, f32[32,5120]{1,0:T(8,128)S(1)} %get-tuple-element.10.first_ref, ...), custom_call_target="tpu_custom_call" | custom-call | tf_op jit(solution)/shard_map/update/pallas_call | solution.py:314
Async XLA Ops:
  0.6 0.7 %copy-start.1 = (f32[16]{0:T(128)S(1)}, f32[16]{0:T(128)}, u32[]{:S(2)}) copy-start(f32[16]{0:T(128)} %weight_hbm.1) | copy-start | bytes 196
  1.3 1.0 %copy-start = (bf16[1,32,5120]{2,1,0:T(8,128)(2,1)S(1)}, bf16[1,32,5120]{2,1,0:T(8,128)(2,1)}, u32[]{:S(2)}) copy-start(bf16[1,32,5120]{2,1,0:T(8,128)(2,1)} %param.5) | copy-start | bytes 983044

commit v3 on v2

--- a/solution.py
+++ b/solution.py
@@ -20,6 +20,12 @@
 
 MESH = pl.DeviceIdType.MESH
 LANES = 128
+PIECES = 1
+GATHER = ({4: 0, 2: 0, 1: 0, 3: 0, 6: 4, 5: 4, 7: 4}, 1)
+
+
+def depth_of(tree, offset):
+    return 0 if offset == 0 else 1 + depth_of(tree, tree[offset])
 
 
 def packed_gram(block, groups, rows):
@@ -66,13 +72,13 @@
 
 
 def kernel(
-    chips, grid, entries, grad_ref, weight_hbm, params_hbm, first_hbm, second_hbm,
+    chips, grid, entries, grad_hbm, weight_hbm, params_hbm, first_hbm, second_hbm,
     out_ref, params_ref, first_ref, second_ref,
-    weight_ref, held, core_small, plane_small, ring_small, core_slot, plane_slots, ring_slots,
-    up, down, beside_sem, near_row, next_row, far_row,
-    weight_sem, copy_sem, held_send, held_recv, core_sem, core_sum_recv,
+    grad_ref, weight_ref, held, core_small, plane_small, ring_small, core_slot, plane_slots, ring_slots,
+    reached, beside_sem, near_row, next_row, far_row,
+    grad_sem, weight_sem, copy_sem, held_send, held_recv, core_sem, core_sum_recv,
     plane_send, plane_recv, ring_send, ring_recv,
-    far_send, chip_send, chip_recv, core_send, core_recv,
+    chip_send, chip_recv, core_send, core_recv,
 ):
     rows_y, runs, rows_x = grid
     groups, plane, ring = 2 * chips, rows_x * rows_y, runs * chips
@@ -92,6 +98,9 @@
             "fsdp": (to_y * runs + lax.div(to_z, chips)) * rows_x + to_x,
         }
 
+    def hops(step, size):
+        return min(step, size - step)
+
     def steps(size):
         return {1: (), 2: (1,)}.get(size, (1, -1))
 
@@ -106,11 +115,13 @@
     def await_bytes(ref, sem):
         pltpu.make_async_copy(ref, ref, sem).wait()
 
+    grad_copy = pltpu.make_async_copy(grad_hbm, grad_ref, grad_sem)
+    grad_copy.start()
     weight_copy = pltpu.make_async_copy(weight_hbm, weight_ref, weight_sem)
     weight_copy.start()
 
     barrier = pltpu.get_barrier_semaphore()
-    greeted = [device(dz=dz, other=other) for dz in steps(ring) for other in (False, True)]
+    greeted = [device(dz=dz, other=other) for dz in (-2, -1, 1, 2) for other in (False, True)]
     greeted += [device(dy=dy) for dy in steps(rows_y)] + [device(dx=dx) for dx in steps(rows_x)]
     greeted += [device(other=True)]
     for to in greeted:
@@ -129,28 +140,36 @@
         to = {"replica": to_chip * 2 + to_core}
         send(part_of(grad_ref, to_chip, to_core), own_held, held_send, held_recv, to).start()
 
+    def send_at(distance):
+        @pl.when(chip + distance < chips)
+        def _():
+            send_part(chip + distance, core)
+            send_part(chip + distance, 1 - core)
+
+        @pl.when(chip >= distance)
+        def _():
+            send_part(chip - distance, core)
+            send_part(chip - distance, 1 - core)
+
+    def tell_both(stage, through):
+        tell(reached.at[stage], device(dz=through))
+        tell(reached.at[stage], device(dz=-through))
+
+    tell_both(0, 2)
+    grad_copy.wait()
     send_part(chip, 1 - core)
     pltpu.make_async_copy(part_of(grad_ref, chip, core), own_held, held_recv).start()
-
-    for distance in range(1, ring // 2 + 1):
-        if distance > 1:
-            pl.semaphore_wait(up.at[distance], 1)
-            if 2 * distance < ring:
-                pl.semaphore_wait(down.at[distance], 1)
-        if distance < ring // 2:
-            tell(up.at[distance + 1], device(dz=1))
-            if 2 * distance + 2 < ring:
-                tell(down.at[distance + 1], device(dz=-1))
-        if distance < chips:
-            @pl.when(chip + distance < chips)
-            def _():
-                send_part(chip + distance, core)
-                send_part(chip + distance, 1 - core)
-
-            @pl.when(chip >= distance)
-            def _():
-                send_part(chip - distance, core)
-                send_part(chip - distance, 1 - core)
+    send_at(1)
+    send_at(2)
+    pl.semaphore_wait(reached.at[0], 2)
+    tell_both(1, 3)
+    send_at(3)
+    send_at(4)
+    pl.semaphore_wait(reached.at[1], 2)
+    tell_both(2, 1)
+    send_at(5)
+    send_at(6)
+    send_at(7)
 
     if rows_x > 2:
         tell(beside_sem, device(dx=1))
@@ -162,6 +181,7 @@
     if rows_y > 2:
         tell(far_row, device(dy=1))
         pl.semaphore_wait(far_row, 1)
+    pl.semaphore_wait(reached.at[2], 2)
 
     kept = [
         pltpu.make_async_copy(params_hbm, params_ref, copy_sem.at[0]),
@@ -181,18 +201,18 @@
     plane_small[...] = core_small[...] + core_slot[...]
 
     if plane > 1:
-        for step in range(1, plane):
+        pltpu.make_async_copy(plane_small, plane_slots.at[y * rows_x + x], plane_recv).start()
+        for step in sorted(range(1, plane), key=lambda step: -hops(step % rows_x, rows_x) - hops(step // rows_x, rows_y)):
             to = device(dx=step % rows_x, dy=step // rows_x)
             send(plane_small, plane_slots.at[y * rows_x + x], plane_send, plane_recv, to).start()
-        pltpu.make_async_copy(plane_small, plane_slots.at[y * rows_x + x], plane_recv).start()
         await_bytes(plane_slots, plane_recv)
         ring_small[...] = jnp.sum(plane_slots[...], axis=0)
     else:
         ring_small[...] = plane_small[...]
 
-    for step in range(1, ring):
+    pltpu.make_async_copy(ring_small, ring_slots.at[z], ring_recv).start()
+    for step in sorted(range(1, ring), key=lambda step: -hops(step, ring)):
         send(ring_small, ring_slots.at[z], ring_send, ring_recv, device(dz=step)).start()
-    pltpu.make_async_copy(ring_small, ring_slots.at[z], ring_recv).start()
     await_bytes(ring_slots, ring_recv)
     weights = median_weights(jnp.sum(ring_slots[...], axis=0), weight_ref, groups, entries)
 
@@ -202,43 +222,57 @@
     part_of(out_ref, chip, core)[...] = total
 
     sibling = {"replica": chip * 2 + 1 - core}
-    beside = chip + 1 - 2 * lax.rem(chip, 2)
-    parity = lax.rem(chip, 2)
-    pairs = chips // 2
-
-    def far(step):
-        return lax.rem(lax.div(chip, 2) + step, pairs) * 2 + parity
-
-    def to_chip(origin, target, send_sem):
-        part = part_of(out_ref, origin, core)
-        return send(part, part, send_sem, chip_recv.at[origin], {"replica": target * 2 + core})
-
-    def to_core(origin, origin_core):
-        part = part_of(out_ref, origin, origin_core)
-        return send(part, part, core_send.at[origin], core_recv.at[origin], sibling)
-
-    for step in range(1, pairs):
-        to_chip(chip, far(step), far_send.at[step]).start()
-    to_chip(chip, beside, chip_send.at[chip]).start()
-    to_core(chip, core).start()
-    for step in range(1, pairs):
-        origin = far(pairs - step)
-        to_chip(origin, beside, chip_send.at[origin]).wait_recv()
-        to_chip(origin, beside, chip_send.at[origin]).start()
-        to_core(origin, core).start()
-    for step in range(pairs):
-        origin = far(step) + 1 - 2 * parity
-        to_chip(origin, beside, chip_send.at[origin]).wait_recv()
-        to_core(origin, core).start()
-    for origin in range(chips):
-        to_core(origin, 1 - core).wait_recv()
-
-    for origin in range(chips):
-        to_core(origin, core).wait_send()
-    for step in range(pairs):
-        to_chip(far(step), beside, chip_send.at[far(step)]).wait_send()
-    for step in range(1, pairs):
-        to_chip(chip, far(step), far_send.at[step]).wait_send()
+    tree, pieces = GATHER
+    cut = rows // pieces
+    place = [chip]
+    for offset in range(1, chips):
+        top = 1 << (offset.bit_length() - 1)
+        below = place[offset - top]
+        place.append(below + top - 2 * top * lax.rem(lax.div(below, top), 2))
+
+    def piece_of(offset, piece, from_core):
+        return out_ref.at[
+            pl.ds(pl.multiple_of(from_core * rows + piece * cut, cut), cut),
+            pl.ds(pl.multiple_of(place[offset] * wide, wide), wide),
+        ]
+
+    def to_chip(child, piece):
+        parent = tree[child]
+        part = piece_of(parent, piece, core)
+        to = {"replica": place[parent ^ child] * 2 + core}
+        return send(part, part, chip_send.at[child, piece], chip_recv.at[child, piece], to)
+
+    def from_chip(child, piece):
+        part = piece_of(child, piece, core)
+        return pltpu.make_async_copy(part, part, chip_recv.at[child, piece])
+
+    def to_core(offset, piece, from_core):
+        part = piece_of(offset, piece, from_core)
+        return send(part, part, core_send.at[offset, piece], core_recv.at[offset, piece], sibling)
+
+    for piece in range(pieces):
+        for child in tree:
+            if tree[child] == 0:
+                to_chip(child, piece).start()
+        to_core(0, piece, core).start()
+    for depth in range(1, 4):
+        for piece in range(pieces):
+            for offset in tree:
+                if depth_of(tree, offset) != depth:
+                    continue
+                from_chip(offset, piece).wait()
+                for child in tree:
+                    if tree[child] == offset:
+                        to_chip(child, piece).start()
+                to_core(offset, piece, core).start()
+    for offset in range(chips):
+        for piece in range(pieces):
+            to_core(offset, piece, 1 - core).wait_recv()
+    for offset in range(chips):
+        for piece in range(pieces):
+            to_core(offset, piece, core).wait_send()
+            if offset > 0:
+                to_chip(offset, piece).wait_send()
     for copy in kept:
         copy.wait()
     await_bytes(held.at[pl.ds(0, (groups - 1) * rows), :], held_send)
@@ -291,25 +325,27 @@
     in_hbm = pl.BlockSpec(memory_space=pltpu.HBM)
     in_vmem = pl.BlockSpec(memory_space=pltpu.VMEM)
     small = pltpu.VMEM((2, LANES), jnp.float32)
+    inputs = (gradients.reshape(rows_here, width), replica_weight, params, first_moment, second_moment)
     gathered = pl.pallas_call(
         functools.partial(kernel, chips, grid, entries),
         out_shape=(whole,) * 4,
         in_specs=[in_hbm] * 5,
         out_specs=(in_vmem,) * 4,
         scratch_shapes=[
+            pltpu.VMEM((rows_here, width), jnp.bfloat16),
             pltpu.SMEM((groups,), jnp.float32),
             pltpu.VMEM((groups * rows, wide), jnp.bfloat16),
             small, small, small, small,
             pltpu.VMEM((rows_x * rows_y, 2, LANES), jnp.float32),
             pltpu.VMEM((ring, 2, LANES), jnp.float32),
-            regular((ring // 2 + 1,)), regular((ring // 2 + 1,)), regular, regular, regular, regular,
-            dma, dma((3,)), dma, dma, dma, dma,
+            regular((3,)), regular, regular, regular, regular,
+            dma, dma, dma((3,)), dma, dma, dma, dma,
             dma, dma, dma, dma,
-            dma((chips // 2,)), dma((chips,)), dma((chips,)), dma((chips,)), dma((chips,)),
+            dma((chips, PIECES)), dma((chips, PIECES)), dma((chips, PIECES)), dma((chips, PIECES)),
         ],
         compiler_params=pltpu.CompilerParams(collective_id=0, has_side_effects=True, vmem_limit_bytes=51 * 1024 * 1024),
         name="median_rows",
-    )(gradients.reshape(rows_here, width), replica_weight, params, first_moment, second_moment)
+    )(*(pltpu.with_memory_space_constraint(array, pltpu.HBM) for array in inputs))
     kept = pltpu.VMEM((rows_here, width), jnp.float32)
     return pl.pallas_call(
         update_kernel,

time: 64 us -> 60.2 us (0.941)
  Pallas kernels: 61.6 us -> 59.4 us
  local copies, waits for them, and re-layouts: 1.62 us -> 0 us
    pallas_call x1, Pallas kernels: 59.8 us -> 57.7 us  [body(): pl.pallas_call(functools.partial(kernel, chips, grid, entries), out_shape...]
    unnamed x4 -> x0, local copies, waits for them, and re-layouts: 1.62 us -> none
where the time goes in v3:
time: 60.2 us; the launch traced here: 60 us
  Pallas kernels  59.4 us (99%)
  between operations  0.64 us (1%)
    pallas_call x1, Pallas kernels, body(): pl.pallas_call(functools.partial(kernel, chips, grid, entries), out_shape...  57.7 us
    pallas_call x1, Pallas kernels, body(): pl.pallas_call(update_kernel, out_shape=(whole,) * 4, in_specs=[in_vmem]...  1.73 us

profile of v3, /device:TPU:1, one launch (start us, length us, event | category | flops | bytes accessed | tf_op | source)
XLA Modules:
  0.0 60.0 jit_solution(781098058777847433)
XLA Ops:
  0.6 57.7 %median_rows.1 = (f32[32,5120]{1,0:T(8,128)S(1)}, f32[32,5120]{1,0:T(8,128)S(1)}, f32[32,5120]{1,0:T(8,128)S(1)}, f32[32,5120]{1,0:T(8,128)S(1)}) custom-call(bf16[32,5120]{1,0:T(8,128)(2,1)} %bitcast.1, f32[16]{0:T(128)} %weight_hbm.1, f32[32,5120]{1,0:T(8,128)} %params_hbm.1, f32[32,5120]{1,0:T(8,128)} %first_hbm.1, f32[32,5120]{1,0:T(8,128)} %second_hbm.1), custom_call_target="tpu_custom_call" | custom-call | tf_op jit(solution)/shard_map/median_rows/pallas_call | solution.py:329
  58.3 1.7 %update.1 = (f32[32,5120]{1,0:T(8,128)}, f32[32,5120]{1,0:T(8,128)}, f32[32,5120]{1,0:T(8,128)}, f32[32,5120]{1,0:T(8,128)}) custom-call(f32[32,5120]{1,0:T(8,128)S(1)} %get-tuple-element.8.median_ref, f32[32,5120]{1,0:T(8,128)S(1)} %get-tuple-element.9.params_ref, f32[32,5120]{1,0:T(8,128)S(1)} %get-tuple-element.10.first_ref, ...), custom_call_target="tpu_custom_call" | custom-call | tf_op jit(solution)/shard_map/update/pallas_call | solution.py:350

commit v4 on v3

--- a/solution.py
+++ b/solution.py
@@ -20,12 +20,14 @@
 
 MESH = pl.DeviceIdType.MESH
 LANES = 128
-PIECES = 1
-GATHER = ({4: 0, 2: 0, 1: 0, 3: 0, 6: 4, 5: 4, 7: 4}, 1)
+SPREAD = {4: 0, 2: 0, 1: 0, 3: 0, 6: 4, 5: 4, 7: 4}
+SPREAD_TWICE = {1: 0, 2: 0, 3: 0, 5: 4, 6: 4, 7: 4}
+TWICE_LANES = 384
+MIRROR_AT = 1
 
 
 def depth_of(tree, offset):
-    return 0 if offset == 0 else 1 + depth_of(tree, tree[offset])
+    return 0 if offset not in tree else 1 + depth_of(tree, tree[offset])
 
 
 def packed_gram(block, groups, rows):
@@ -74,9 +76,9 @@
 def kernel(
     chips, grid, entries, grad_hbm, weight_hbm, params_hbm, first_hbm, second_hbm,
     out_ref, params_ref, first_ref, second_ref,
-    grad_ref, weight_ref, held, core_small, plane_small, ring_small, core_slot, plane_slots, ring_slots,
+    grad_ref, weight_ref, held, held_twice, core_small, plane_small, ring_small, core_slot, plane_slots, ring_slots,
     reached, beside_sem, near_row, next_row, far_row,
-    grad_sem, weight_sem, copy_sem, held_send, held_recv, core_sem, core_sum_recv,
+    grad_sem, weight_sem, copy_sem, held_send, held_recv, twice_send, twice_recv, core_sem, core_sum_recv,
     plane_send, plane_recv, ring_send, ring_recv,
     chip_send, chip_recv, core_send, core_recv,
 ):
@@ -88,6 +90,7 @@
     z = run * chips + chip
     rows = grad_ref.shape[0] // 2
     wide = grad_ref.shape[1] // chips
+    twice = held_twice.shape[1]
 
     def device(dz=0, dy=0, dx=0, other=False):
         to_z = lax.rem(z + dz + ring, ring)
@@ -192,6 +195,26 @@
         copy.start()
     weight_copy.wait()
 
+    across = chip + 4 - 8 * lax.div(chip, 4)
+    own_twice = held_twice.at[pl.ds(pl.multiple_of(replica * rows, rows), rows), :]
+
+    def twice_of(ref, owner_chip, owner_core):
+        return ref.at[
+            pl.ds(pl.multiple_of(owner_core * rows, rows), rows),
+            pl.ds(pl.multiple_of(owner_chip * wide, wide), twice),
+        ]
+
+    def send_twice(step):
+        to = lax.rem(replica + step, groups)
+        to_chip = lax.div(to, 2)
+        src = twice_of(grad_ref, to_chip + 4 - 8 * lax.div(to_chip, 4), lax.rem(to, 2))
+        send(src, own_twice, twice_send, twice_recv, {"replica": to}).start()
+
+    pltpu.make_async_copy(twice_of(grad_ref, across, core), own_twice, twice_recv).start()
+    if MIRROR_AT == 0:
+        for step in range(1, groups):
+            send_twice(step)
+
     await_bytes(held, held_recv)
     core_small[...] = packed_gram(held[...], groups, rows)
 
@@ -205,6 +228,9 @@
         for step in sorted(range(1, plane), key=lambda step: -hops(step % rows_x, rows_x) - hops(step // rows_x, rows_y)):
             to = device(dx=step % rows_x, dy=step // rows_x)
             send(plane_small, plane_slots.at[y * rows_x + x], plane_send, plane_recv, to).start()
+        if MIRROR_AT == 1:
+            for step in range(1, groups):
+                send_twice(step)
         await_bytes(plane_slots, plane_recv)
         ring_small[...] = jnp.sum(plane_slots[...], axis=0)
     else:
@@ -216,14 +242,19 @@
     await_bytes(ring_slots, ring_recv)
     weights = median_weights(jnp.sum(ring_slots[...], axis=0), weight_ref, groups, entries)
 
-    total = jnp.zeros((rows, wide), jnp.float32)
-    for group in range(groups):
-        total += weights[group : group + 1, :1] * held[group * rows : (group + 1) * rows, :].astype(jnp.float32)
-    part_of(out_ref, chip, core)[...] = total
+    def pooled(block, width):
+        total = jnp.zeros((rows, width), jnp.float32)
+        for group in range(groups):
+            total += weights[group : group + 1, :1] * block[group * rows : (group + 1) * rows, :].astype(jnp.float32)
+        return total
+
+    part_of(out_ref, chip, core)[...] = pooled(held, wide)
+    await_bytes(held_twice, twice_recv)
+    twice_of(out_ref, across, core)[...] = pooled(held_twice, twice)
 
     sibling = {"replica": chip * 2 + 1 - core}
-    tree, pieces = GATHER
-    cut = rows // pieces
+    pieces = ((twice, wide - twice, SPREAD), (0, twice, SPREAD_TWICE))
+    pieces = tuple(piece for piece in pieces if piece[1] > 0)
     place = [chip]
     for offset in range(1, chips):
         top = 1 << (offset.bit_length() - 1)
@@ -231,13 +262,14 @@
         place.append(below + top - 2 * top * lax.rem(lax.div(below, top), 2))
 
     def piece_of(offset, piece, from_core):
+        start, width, _ = pieces[piece]
         return out_ref.at[
-            pl.ds(pl.multiple_of(from_core * rows + piece * cut, cut), cut),
-            pl.ds(pl.multiple_of(place[offset] * wide, wide), wide),
+            pl.ds(pl.multiple_of(from_core * rows, rows), rows),
+            pl.ds(pl.multiple_of(place[offset] * wide + start, LANES), width),
         ]
 
     def to_chip(child, piece):
-        parent = tree[child]
+        parent = pieces[piece][2][child]
         part = piece_of(parent, piece, core)
         to = {"replica": place[parent ^ child] * 2 + core}
         return send(part, part, chip_send.at[child, piece], chip_recv.at[child, piece], to)
@@ -250,29 +282,35 @@
         part = piece_of(offset, piece, from_core)
         return send(part, part, core_send.at[offset, piece], core_recv.at[offset, piece], sibling)
 
-    for piece in range(pieces):
-        for child in tree:
-            if tree[child] == 0:
+    def passed_on(offset, piece):
+        for child, parent in pieces[piece][2].items():
+            if parent == offset:
                 to_chip(child, piece).start()
-        to_core(0, piece, core).start()
-    for depth in range(1, 4):
-        for piece in range(pieces):
+
+    for piece, (_, _, tree) in enumerate(pieces):
+        for offset in range(chips):
+            if offset not in tree:
+                passed_on(offset, piece)
+    for piece, (_, _, tree) in enumerate(pieces):
+        for offset in range(chips):
+            if offset not in tree:
+                to_core(offset, piece, core).start()
+    for depth in (1, 2):
+        for piece, (_, _, tree) in enumerate(pieces):
             for offset in tree:
-                if depth_of(tree, offset) != depth:
-                    continue
-                from_chip(offset, piece).wait()
-                for child in tree:
-                    if tree[child] == offset:
-                        to_chip(child, piece).start()
-                to_core(offset, piece, core).start()
-    for offset in range(chips):
-        for piece in range(pieces):
+                if depth_of(tree, offset) == depth:
+                    from_chip(offset, piece).wait()
+                    passed_on(offset, piece)
+                    to_core(offset, piece, core).start()
+    for piece, (_, _, tree) in enumerate(pieces):
+        for offset in range(chips):
             to_core(offset, piece, 1 - core).wait_recv()
-    for offset in range(chips):
-        for piece in range(pieces):
+    for piece, (_, _, tree) in enumerate(pieces):
+        for offset in range(chips):
             to_core(offset, piece, core).wait_send()
-            if offset > 0:
+            if offset in tree:
                 to_chip(offset, piece).wait_send()
+    await_bytes(held_twice.at[pl.ds(0, (groups - 1) * rows), :], twice_send)
     for copy in kept:
         copy.wait()
     await_bytes(held.at[pl.ds(0, (groups - 1) * rows), :], held_send)
@@ -335,13 +373,14 @@
             pltpu.VMEM((rows_here, width), jnp.bfloat16),
             pltpu.SMEM((groups,), jnp.float32),
             pltpu.VMEM((groups * rows, wide), jnp.bfloat16),
+            pltpu.VMEM((groups * rows, TWICE_LANES), jnp.bfloat16),
             small, small, small, small,
             pltpu.VMEM((rows_x * rows_y, 2, LANES), jnp.float32),
             pltpu.VMEM((ring, 2, LANES), jnp.float32),
             regular((3,)), regular, regular, regular, regular,
-            dma, dma, dma((3,)), dma, dma, dma, dma,
+            dma, dma, dma((3,)), dma, dma, dma, dma, dma, dma,
             dma, dma, dma, dma,
-            dma((chips, PIECES)), dma((chips, PIECES)), dma((chips, PIECES)), dma((chips, PIECES)),
+            dma((chips, 2)), dma((chips, 2)), dma((chips, 2)), dma((chips, 2)),
         ],
         compiler_params=pltpu.CompilerParams(collective_id=0, has_side_effects=True, vmem_limit_bytes=51 * 1024 * 1024),
         name="median_rows",

time: 60.2 us -> 59.4 us (0.987)
  Pallas kernels: 59.4 us -> 58.6 us
    pallas_call x1, Pallas kernels: 57.7 us -> 56.9 us  [body(): pl.pallas_call(functools.partial(kernel, chips, grid, entries), out_shape...]
where the time goes in v4:
time: 59.4 us; the launch traced here: 59.3 us
  Pallas kernels  58.6 us (99%)
  between operations  0.64 us (1%)
    pallas_call x1, Pallas kernels, body(): pl.pallas_call(functools.partial(kernel, chips, grid, entries), out_shape...  56.9 us
    pallas_call x1, Pallas kernels, body(): pl.pallas_call(update_kernel, out_shape=(whole,) * 4, in_specs=[in_vmem]...  1.73 us

profile of v4, /device:TPU:1, one launch (start us, length us, event | category | flops | bytes accessed | tf_op | source)
XLA Modules:
  0.0 59.3 jit_solution(7709716704459380238)
XLA Ops:
  0.6 56.9 %median_rows.1 = (f32[32,5120]{1,0:T(8,128)S(1)}, f32[32,5120]{1,0:T(8,128)S(1)}, f32[32,5120]{1,0:T(8,128)S(1)}, f32[32,5120]{1,0:T(8,128)S(1)}) custom-call(bf16[32,5120]{1,0:T(8,128)(2,1)} %bitcast.1, f32[16]{0:T(128)} %weight_hbm.1, f32[32,5120]{1,0:T(8,128)} %params_hbm.1, f32[32,5120]{1,0:T(8,128)} %first_hbm.1, f32[32,5120]{1,0:T(8,128)} %second_hbm.1), custom_call_target="tpu_custom_call" | custom-call | tf_op jit(solution)/shard_map/median_rows/pallas_call | solution.py:367
  57.5 1.7 %update.1 = (f32[32,5120]{1,0:T(8,128)}, f32[32,5120]{1,0:T(8,128)}, f32[32,5120]{1,0:T(8,128)}, f32[32,5120]{1,0:T(8,128)}) custom-call(f32[32,5120]{1,0:T(8,128)S(1)} %get-tuple-element.8.median_ref, f32[32,5120]{1,0:T(8,128)S(1)} %get-tuple-element.9.params_ref, f32[32,5120]{1,0:T(8,128)S(1)} %get-tuple-element.10.first_ref, ...), custom_call_target="tpu_custom_call" | custom-call | tf_op jit(solution)/shard_map/update/pallas_call | solution.py:389

commit v5 on v4

--- a/solution.py
+++ b/solution.py
@@ -23,11 +23,7 @@
 SPREAD = {4: 0, 2: 0, 1: 0, 3: 0, 6: 4, 5: 4, 7: 4}
 SPREAD_TWICE = {1: 0, 2: 0, 3: 0, 5: 4, 6: 4, 7: 4}
 TWICE_LANES = 384
-MIRROR_AT = 1
-
-
-def depth_of(tree, offset):
-    return 0 if offset not in tree else 1 + depth_of(tree, tree[offset])
+ARRIVALS = [(0, 4), (0, 2), (0, 1), (0, 3), (1, 1), (1, 2), (1, 3), (1, 5), (1, 6), (1, 7), (0, 6), (0, 5), (0, 7)]
 
 
 def packed_gram(block, groups, rows):
@@ -76,9 +72,9 @@
 def kernel(
     chips, grid, entries, grad_hbm, weight_hbm, params_hbm, first_hbm, second_hbm,
     out_ref, params_ref, first_ref, second_ref,
-    grad_ref, weight_ref, held, held_twice, core_small, plane_small, ring_small, core_slot, plane_slots, ring_slots,
-    reached, beside_sem, near_row, next_row, far_row,
-    grad_sem, weight_sem, copy_sem, held_send, held_recv, twice_send, twice_recv, core_sem, core_sum_recv,
+    grad_ref, weight_ref, held, held_twice, plane_small, ring_small, plane_slots, ring_slots,
+    reached, both_sem, beside_sem, near_row, next_row, far_row,
+    grad_sem, weight_sem, copy_sem, held_send, held_recv, twice_send, twice_recv,
     plane_send, plane_recv, ring_send, ring_recv,
     chip_send, chip_recv, core_send, core_recv,
 ):
@@ -174,6 +170,10 @@
     send_at(6)
     send_at(7)
 
+    for dx in steps(rows_x):
+        tell(both_sem, device(dx=dx))
+    if rows_x > 1:
+        pl.semaphore_wait(both_sem, len(steps(rows_x)))
     if rows_x > 2:
         tell(beside_sem, device(dx=1))
         pl.semaphore_wait(beside_sem, 1)
@@ -211,30 +211,22 @@
         send(src, own_twice, twice_send, twice_recv, {"replica": to}).start()
 
     pltpu.make_async_copy(twice_of(grad_ref, across, core), own_twice, twice_recv).start()
-    if MIRROR_AT == 0:
-        for step in range(1, groups):
-            send_twice(step)
 
     await_bytes(held, held_recv)
-    core_small[...] = packed_gram(held[...], groups, rows)
-
-    exchange = send(core_small, core_slot, core_sem, core_sum_recv, device(other=True))
-    exchange.start()
-    exchange.wait()
-    plane_small[...] = core_small[...] + core_slot[...]
-
-    if plane > 1:
-        pltpu.make_async_copy(plane_small, plane_slots.at[y * rows_x + x], plane_recv).start()
-        for step in sorted(range(1, plane), key=lambda step: -hops(step % rows_x, rows_x) - hops(step // rows_x, rows_y)):
-            to = device(dx=step % rows_x, dy=step // rows_x)
-            send(plane_small, plane_slots.at[y * rows_x + x], plane_send, plane_recv, to).start()
-        if MIRROR_AT == 1:
-            for step in range(1, groups):
-                send_twice(step)
-        await_bytes(plane_slots, plane_recv)
-        ring_small[...] = jnp.sum(plane_slots[...], axis=0)
-    else:
-        ring_small[...] = plane_small[...]
+    plane_small[...] = packed_gram(held[...], groups, rows)
+
+    own_slot = plane_slots.at[(y * rows_x + x) * 2 + core]
+    pltpu.make_async_copy(plane_small, own_slot, plane_recv).start()
+    far_first = sorted(range(plane), key=lambda step: -hops(step % rows_x, rows_x) - hops(step // rows_x, rows_y))
+    for step in far_first:
+        for other in (False, True):
+            if step > 0 or other:
+                to = device(dx=step % rows_x, dy=step // rows_x, other=other)
+                send(plane_small, own_slot, plane_send, plane_recv, to).start()
+    for step in range(1, groups):
+        send_twice(step)
+    await_bytes(plane_slots, plane_recv)
+    ring_small[...] = jnp.sum(plane_slots[...], axis=0)
 
     pltpu.make_async_copy(ring_small, ring_slots.at[z], ring_recv).start()
     for step in sorted(range(1, ring), key=lambda step: -hops(step, ring)):
@@ -249,12 +241,9 @@
         return total
 
     part_of(out_ref, chip, core)[...] = pooled(held, wide)
-    await_bytes(held_twice, twice_recv)
-    twice_of(out_ref, across, core)[...] = pooled(held_twice, twice)
 
     sibling = {"replica": chip * 2 + 1 - core}
     pieces = ((twice, wide - twice, SPREAD), (0, twice, SPREAD_TWICE))
-    pieces = tuple(piece for piece in pieces if piece[1] > 0)
     place = [chip]
     for offset in range(1, chips):
         top = 1 << (offset.bit_length() - 1)
@@ -287,21 +276,18 @@
             if parent == offset:
                 to_chip(child, piece).start()
 
-    for piece, (_, _, tree) in enumerate(pieces):
-        for offset in range(chips):
-            if offset not in tree:
-                passed_on(offset, piece)
-    for piece, (_, _, tree) in enumerate(pieces):
-        for offset in range(chips):
-            if offset not in tree:
-                to_core(offset, piece, core).start()
-    for depth in (1, 2):
-        for piece, (_, _, tree) in enumerate(pieces):
-            for offset in tree:
-                if depth_of(tree, offset) == depth:
-                    from_chip(offset, piece).wait()
-                    passed_on(offset, piece)
-                    to_core(offset, piece, core).start()
+    for piece in range(2):
+        passed_on(0, piece)
+    for piece in range(2):
+        to_core(0, piece, core).start()
+    await_bytes(held_twice, twice_recv)
+    twice_of(out_ref, across, core)[...] = pooled(held_twice, twice)
+    passed_on(4, 1)
+    to_core(4, 1, core).start()
+    for piece, offset in ARRIVALS:
+        from_chip(offset, piece).wait()
+        passed_on(offset, piece)
+        to_core(offset, piece, core).start()
     for piece, (_, _, tree) in enumerate(pieces):
         for offset in range(chips):
             to_core(offset, piece, 1 - core).wait_recv()
@@ -314,8 +300,7 @@
     for copy in kept:
         copy.wait()
     await_bytes(held.at[pl.ds(0, (groups - 1) * rows), :], held_send)
-    if plane > 1:
-        await_bytes(plane_slots.at[pl.ds(0, plane - 1)], plane_send)
+    await_bytes(plane_slots.at[pl.ds(0, 2 * plane - 1)], plane_send)
     await_bytes(ring_slots.at[pl.ds(0, ring - 1)], ring_send)
 
 
@@ -374,11 +359,11 @@
             pltpu.SMEM((groups,), jnp.float32),
             pltpu.VMEM((groups * rows, wide), jnp.bfloat16),
             pltpu.VMEM((groups * rows, TWICE_LANES), jnp.bfloat16),
-            small, small, small, small,
-            pltpu.VMEM((rows_x * rows_y, 2, LANES), jnp.float32),
+            small, small,
+            pltpu.VMEM((2 * rows_x * rows_y, 2, LANES), jnp.float32),
             pltpu.VMEM((ring, 2, LANES), jnp.float32),
-            regular((3,)), regular, regular, regular, regular,
-            dma, dma, dma((3,)), dma, dma, dma, dma, dma, dma,
+            regular((3,)), regular, regular, regular, regular, regular,
+            dma, dma, dma((3,)), dma, dma, dma, dma,
             dma, dma, dma, dma,
             dma((chips, 2)), dma((chips, 2)), dma((chips, 2)), dma((chips, 2)),
         ],

time: 59.4 us -> 58.5 us (0.985)
  Pallas kernels: 58.6 us -> 57.7 us
    pallas_call x1, Pallas kernels: 56.9 us -> 56 us  [body(): pl.pallas_call(functools.partial(kernel, chips, grid, entries), out_shape...]
where the time goes in v5:
time: 58.5 us; the launch traced here: 58.4 us
  Pallas kernels  57.7 us (99%)
  between operations  0.64 us (1%)
    pallas_call x1, Pallas kernels, body(): pl.pallas_call(functools.partial(kernel, chips, grid, entries), out_shape...  56 us
    pallas_call x1, Pallas kernels, body(): pl.pallas_call(update_kernel, out_shape=(whole,) * 4, in_specs=[in_vmem]...  1.73 us

profile of v5, /device:TPU:1, one launch (start us, length us, event | category | flops | bytes accessed | tf_op | source)
XLA Modules:
  0.0 58.4 jit_solution(7900812135385813342)
XLA Ops:
  0.6 56.0 %median_rows.1 = (f32[32,5120]{1,0:T(8,128)S(1)}, f32[32,5120]{1,0:T(8,128)S(1)}, f32[32,5120]{1,0:T(8,128)S(1)}, f32[32,5120]{1,0:T(8,128)S(1)}) custom-call(bf16[32,5120]{1,0:T(8,128)(2,1)} %bitcast.1, f32[16]{0:T(128)} %weight_hbm.1, f32[32,5120]{1,0:T(8,128)} %params_hbm.1, f32[32,5120]{1,0:T(8,128)} %first_hbm.1, f32[32,5120]{1,0:T(8,128)} %second_hbm.1), custom_call_target="tpu_custom_call" | custom-call | tf_op jit(solution)/shard_map/median_rows/pallas_call | solution.py:352
  56.7 1.7 %update.1 = (f32[32,5120]{1,0:T(8,128)}, f32[32,5120]{1,0:T(8,128)}, f32[32,5120]{1,0:T(8,128)}, f32[32,5120]{1,0:T(8,128)}) custom-call(f32[32,5120]{1,0:T(8,128)S(1)} %get-tuple-element.8.median_ref, f32[32,5120]{1,0:T(8,128)S(1)} %get-tuple-element.9.params_ref, f32[32,5120]{1,0:T(8,128)S(1)} %get-tuple-element.10.first_ref, ...), custom_call_target="tpu_custom_call" | custom-call | tf_op jit(solution)/shard_map/update/pallas_call | solution.py:374

commit v6 on v5

--- a/solution.py
+++ b/solution.py
@@ -114,17 +114,16 @@
     def await_bytes(ref, sem):
         pltpu.make_async_copy(ref, ref, sem).wait()
 
-    grad_copy = pltpu.make_async_copy(grad_hbm, grad_ref, grad_sem)
-    grad_copy.start()
-    weight_copy = pltpu.make_async_copy(weight_hbm, weight_ref, weight_sem)
-    weight_copy.start()
-
     barrier = pltpu.get_barrier_semaphore()
     greeted = [device(dz=dz, other=other) for dz in (-2, -1, 1, 2) for other in (False, True)]
     greeted += [device(dy=dy) for dy in steps(rows_y)] + [device(dx=dx) for dx in steps(rows_x)]
     greeted += [device(other=True)]
     for to in greeted:
         tell(barrier, to)
+    grad_copy = pltpu.make_async_copy(grad_hbm, grad_ref, grad_sem)
+    grad_copy.start()
+    weight_copy = pltpu.make_async_copy(weight_hbm, weight_ref, weight_sem)
+    weight_copy.start()
     pl.semaphore_wait(barrier, len(greeted))
 
     def part_of(ref, owner_chip, owner_core):
@@ -261,15 +260,15 @@
         parent = pieces[piece][2][child]
         part = piece_of(parent, piece, core)
         to = {"replica": place[parent ^ child] * 2 + core}
-        return send(part, part, chip_send.at[child, piece], chip_recv.at[child, piece], to)
+        return send(part, part, chip_send, chip_recv.at[child, piece], to)
 
     def from_chip(child, piece):
         part = piece_of(child, piece, core)
         return pltpu.make_async_copy(part, part, chip_recv.at[child, piece])
 
-    def to_core(offset, piece, from_core):
-        part = piece_of(offset, piece, from_core)
-        return send(part, part, core_send.at[offset, piece], core_recv.at[offset, piece], sibling)
+    def to_core(offset, piece):
+        part = piece_of(offset, piece, core)
+        return send(part, part, core_send, core_recv, sibling)
 
     def passed_on(offset, piece):
         for child, parent in pieces[piece][2].items():
@@ -279,29 +278,25 @@
     for piece in range(2):
         passed_on(0, piece)
     for piece in range(2):
-        to_core(0, piece, core).start()
+        to_core(0, piece).start()
     await_bytes(held_twice, twice_recv)
     twice_of(out_ref, across, core)[...] = pooled(held_twice, twice)
     passed_on(4, 1)
-    to_core(4, 1, core).start()
-    for piece, offset in ARRIVALS:
-        from_chip(offset, piece).wait()
-        passed_on(offset, piece)
-        to_core(offset, piece, core).start()
-    for piece, (_, _, tree) in enumerate(pieces):
-        for offset in range(chips):
-            to_core(offset, piece, 1 - core).wait_recv()
-    for piece, (_, _, tree) in enumerate(pieces):
-        for offset in range(chips):
-            to_core(offset, piece, core).wait_send()
-            if offset in tree:
-                to_chip(offset, piece).wait_send()
-    await_bytes(held_twice.at[pl.ds(0, (groups - 1) * rows), :], twice_send)
+    to_core(4, 1).start()
     for copy in kept:
         copy.wait()
     await_bytes(held.at[pl.ds(0, (groups - 1) * rows), :], held_send)
     await_bytes(plane_slots.at[pl.ds(0, 2 * plane - 1)], plane_send)
     await_bytes(ring_slots.at[pl.ds(0, ring - 1)], ring_send)
+    for piece, offset in ARRIVALS:
+        from_chip(offset, piece).wait()
+        passed_on(offset, piece)
+        to_core(offset, piece).start()
+    sent = sum(width * len(tree) for _, width, tree in pieces)
+    await_bytes(out_ref.at[pl.ds(0, rows), pl.ds(0, sent)], chip_send)
+    await_bytes(held_twice.at[pl.ds(0, (groups - 1) * rows), :], twice_send)
+    await_bytes(out_ref.at[pl.ds(pl.multiple_of(core * rows, rows), rows), :], core_send)
+    await_bytes(out_ref.at[pl.ds(pl.multiple_of((1 - core) * rows, rows), rows), :], core_recv)
 
 
 def update_kernel(
@@ -365,7 +360,7 @@
             regular((3,)), regular, regular, regular, regular, regular,
             dma, dma, dma((3,)), dma, dma, dma, dma,
             dma, dma, dma, dma,
-            dma((chips, 2)), dma((chips, 2)), dma((chips, 2)), dma((chips, 2)),
+            dma, dma((chips, 2)), dma, dma,
         ],
         compiler_params=pltpu.CompilerParams(collective_id=0, has_side_effects=True, vmem_limit_bytes=51 * 1024 * 1024),
         name="median_rows",

time: 58.5 us -> 58 us (level)
  no operation moved by 1% of the time
where the time goes in v6:
time: 58 us; the launch traced here: 57.9 us
  Pallas kernels  57.3 us (99%)
  between operations  0.64 us (1%)
    pallas_call x1, Pallas kernels, body(): pl.pallas_call(functools.partial(kernel, chips, grid, entries), out_shape...  55.5 us
    pallas_call x1, Pallas kernels, body(): pl.pallas_call(update_kernel, out_shape=(whole,) * 4, in_specs=[in_vmem]...  1.73 us

profile of v6, /device:TPU:1, one launch (start us, length us, event | category | flops | bytes accessed | tf_op | source)
XLA Modules:
  0.0 57.9 jit_solution(1317466123119626479)
XLA Ops:
  0.6 55.5 %median_rows.1 = (f32[32,5120]{1,0:T(8,128)S(1)}, f32[32,5120]{1,0:T(8,128)S(1)}, f32[32,5120]{1,0:T(8,128)S(1)}, f32[32,5120]{1,0:T(8,128)S(1)}) custom-call(bf16[32,5120]{1,0:T(8,128)(2,1)} %bitcast.1, f32[16]{0:T(128)} %weight_hbm.1, f32[32,5120]{1,0:T(8,128)} %params_hbm.1, f32[32,5120]{1,0:T(8,128)} %first_hbm.1, f32[32,5120]{1,0:T(8,128)} %second_hbm.1), custom_call_target="tpu_custom_call" | custom-call | tf_op jit(solution)/shard_map/median_rows/pallas_call | solution.py:347
  56.2 1.7 %update.1 = (f32[32,5120]{1,0:T(8,128)}, f32[32,5120]{1,0:T(8,128)}, f32[32,5120]{1,0:T(8,128)}, f32[32,5120]{1,0:T(8,128)}) custom-call(f32[32,5120]{1,0:T(8,128)S(1)} %get-tuple-element.8.median_ref, f32[32,5120]{1,0:T(8,128)S(1)} %get-tuple-element.9.params_ref, f32[32,5120]{1,0:T(8,128)S(1)} %get-tuple-element.10.first_ref, ...), custom_call_target="tpu_custom_call" | custom-call | tf_op jit(solution)/shard_map/update/pallas_call | solution.py:369

commit v7 on v6

--- a/solution.py
+++ b/solution.py
@@ -45,7 +45,15 @@
     return fold(folded[:2], folded[2:], 1)
 
 
-def median_weights(packed, weight_ref, groups, entries):
+def given_weights(weight_ref, groups):
+    sub = lax.broadcasted_iota(jnp.int32, (groups, LANES), 0)
+    given = jnp.zeros((groups, LANES), jnp.float32)
+    for group in range(groups):
+        given = jnp.where(sub == group, weight_ref[group], given)
+    return given
+
+
+def median_weights(packed, given, groups, entries):
     lane = lax.broadcasted_iota(jnp.int32, (groups, LANES), 1)
     sub = lax.broadcasted_iota(jnp.int32, (groups, LANES), 0)
     lane_group = lax.div(lane, 16) + 8 * lax.div(lax.rem(lane, 16), 8)
@@ -53,9 +61,6 @@
     both = jnp.where(lax.rem(sub, 2) == 0, packed[:1], packed[1:])
     gram = jnp.where(here, both, 0.0) * (1.0 / entries)
     own_lane = lane_group == sub
-    given = jnp.zeros((groups, LANES), jnp.float32)
-    for group in range(groups):
-        given = jnp.where(sub == group, weight_ref[group], given)
     norm = jnp.sum(jnp.where(own_lane, gram, 0.0), axis=1, keepdims=True)
     weight = given
     for iteration in range(ITERS + 1):
@@ -138,16 +143,16 @@
         to = {"replica": to_chip * 2 + to_core}
         send(part_of(grad_ref, to_chip, to_core), own_held, held_send, held_recv, to).start()
 
-    def send_at(distance):
+    def send_at(distance, send_one=send_part):
         @pl.when(chip + distance < chips)
         def _():
-            send_part(chip + distance, core)
-            send_part(chip + distance, 1 - core)
+            send_one(chip + distance, core)
+            send_one(chip + distance, 1 - core)
 
         @pl.when(chip >= distance)
         def _():
-            send_part(chip - distance, core)
-            send_part(chip - distance, 1 - core)
+            send_one(chip - distance, core)
+            send_one(chip - distance, 1 - core)
 
     def tell_both(stage, through):
         tell(reached.at[stage], device(dz=through))
@@ -203,11 +208,9 @@
             pl.ds(pl.multiple_of(owner_chip * wide, wide), twice),
         ]
 
-    def send_twice(step):
-        to = lax.rem(replica + step, groups)
-        to_chip = lax.div(to, 2)
-        src = twice_of(grad_ref, to_chip + 4 - 8 * lax.div(to_chip, 4), lax.rem(to, 2))
-        send(src, own_twice, twice_send, twice_recv, {"replica": to}).start()
+    def send_twice(to_chip, to_core):
+        src = twice_of(grad_ref, to_chip + 4 - 8 * lax.div(to_chip, 4), to_core)
+        send(src, own_twice, twice_send, twice_recv, {"replica": to_chip * 2 + to_core}).start()
 
     pltpu.make_async_copy(twice_of(grad_ref, across, core), own_twice, twice_recv).start()
 
@@ -222,24 +225,25 @@
             if step > 0 or other:
                 to = device(dx=step % rows_x, dy=step // rows_x, other=other)
                 send(plane_small, own_slot, plane_send, plane_recv, to).start()
-    for step in range(1, groups):
-        send_twice(step)
+    send_twice(chip, 1 - core)
+    for distance in range(1, chips):
+        send_at(distance, send_twice)
     await_bytes(plane_slots, plane_recv)
     ring_small[...] = jnp.sum(plane_slots[...], axis=0)
 
     pltpu.make_async_copy(ring_small, ring_slots.at[z], ring_recv).start()
     for step in sorted(range(1, ring), key=lambda step: -hops(step, ring)):
         send(ring_small, ring_slots.at[z], ring_send, ring_recv, device(dz=step)).start()
+    given = given_weights(weight_ref, groups)
     await_bytes(ring_slots, ring_recv)
-    weights = median_weights(jnp.sum(ring_slots[...], axis=0), weight_ref, groups, entries)
-
-    def pooled(block, width):
+    weights = median_weights(jnp.sum(ring_slots[...], axis=0), given, groups, entries)
+
+    def pooled(block, start, width):
         total = jnp.zeros((rows, width), jnp.float32)
         for group in range(groups):
-            total += weights[group : group + 1, :1] * block[group * rows : (group + 1) * rows, :].astype(jnp.float32)
+            part = block[group * rows : (group + 1) * rows, start : start + width]
+            total += weights[group : group + 1, :1] * part.astype(jnp.float32)
         return total
-
-    part_of(out_ref, chip, core)[...] = pooled(held, wide)
 
     sibling = {"replica": chip * 2 + 1 - core}
     pieces = ((twice, wide - twice, SPREAD), (0, twice, SPREAD_TWICE))
@@ -275,12 +279,13 @@
             if parent == offset:
                 to_chip(child, piece).start()
 
-    for piece in range(2):
+    for piece, (start, width, _) in enumerate(pieces):
+        piece_of(0, piece, core)[...] = pooled(held, start, width)
         passed_on(0, piece)
     for piece in range(2):
         to_core(0, piece).start()
     await_bytes(held_twice, twice_recv)
-    twice_of(out_ref, across, core)[...] = pooled(held_twice, twice)
+    twice_of(out_ref, across, core)[...] = pooled(held_twice, 0, twice)
     passed_on(4, 1)
     to_core(4, 1).start()
     for copy in kept:

time: 58 us -> 58 us (level)
  no operation moved by 1% of the time
where the time goes in v7:
time: 58 us; the launch traced here: 57.9 us
  Pallas kernels  57.2 us (99%)
  between operations  0.64 us (1%)
    pallas_call x1, Pallas kernels, body(): pl.pallas_call(functools.partial(kernel, chips, grid, entries), out_shape...  55.5 us
    pallas_call x1, Pallas kernels, body(): pl.pallas_call(update_kernel, out_shape=(whole,) * 4, in_specs=[in_vmem]...  1.73 us

profile of v7, /device:TPU:1, one launch (start us, length us, event | category | flops | bytes accessed | tf_op | source)
XLA Modules:
  0.0 57.9 jit_solution(1705007185958440204)
XLA Ops:
  0.6 55.5 %median_rows.1 = (f32[32,5120]{1,0:T(8,128)S(1)}, f32[32,5120]{1,0:T(8,128)S(1)}, f32[32,5120]{1,0:T(8,128)S(1)}, f32[32,5120]{1,0:T(8,128)S(1)}) custom-call(bf16[32,5120]{1,0:T(8,128)(2,1)} %bitcast.1, f32[16]{0:T(128)} %weight_hbm.1, f32[32,5120]{1,0:T(8,128)} %params_hbm.1, f32[32,5120]{1,0:T(8,128)} %first_hbm.1, f32[32,5120]{1,0:T(8,128)} %second_hbm.1), custom_call_target="tpu_custom_call" | custom-call | tf_op jit(solution)/shard_map/median_rows/pallas_call | solution.py:352
  56.1 1.7 %update.1 = (f32[32,5120]{1,0:T(8,128)}, f32[32,5120]{1,0:T(8,128)}, f32[32,5120]{1,0:T(8,128)}, f32[32,5120]{1,0:T(8,128)}) custom-call(f32[32,5120]{1,0:T(8,128)S(1)} %get-tuple-element.8.median_ref, f32[32,5120]{1,0:T(8,128)S(1)} %get-tuple-element.9.params_ref, f32[32,5120]{1,0:T(8,128)S(1)} %get-tuple-element.10.first_ref, ...), custom_call_target="tpu_custom_call" | custom-call | tf_op jit(solution)/shard_map/update/pallas_call | solution.py:374
